TPU v7x, 32 devices: a whole 2x2x4 slice. The times are simulated.
32 devices in a mesh: dp: 1, expert: 32 (over z, y, x, core).
Axes of the slice: x: 2, y: 2, z: 4, core: 2. Of those that a mesh axis runs over, the one named last changes fastest.
Arguments:
- tokens_in: bfloat16 [512, 2048], P(('dp', 'expert')), may hold values from -6 to 6
- out_grad: bfloat16 [512, 2048], P(('dp', 'expert')), may hold values from -6 to 6
- chosen: int32 [1, 16, 64], P('dp'), may hold values from 0 to 511, as said below
- counts: int32 [1, 16], P('dp'), may hold values from 48 to 64, as said below
- gates: bfloat16 [1, 16, 64], P('dp'), may hold values from 0.049804688 to 1
- w_up: bfloat16 [32, 2048, 2048], P('expert', None, 'dp'), may hold values from -0.125 to 0.125
- w_down: bfloat16 [32, 2048, 2048], P('expert', 'dp'), may hold values from -0.09375 to 0.09375
Outputs:
- in_grad: bfloat16 [512, 2048], P(('dp', 'expert'))
- grad_up: bfloat16 [32, 2048, 2048], P('expert', None, 'dp')
- grad_down: bfloat16 [32, 2048, 2048], P('expert', 'dp')
- gate_grad: float32 [1, 32, 32], P('dp', 'expert')
Inputs may be any that keep to these rules, and one draw needn't show every extreme that they name: chosen[g, e, c] numbers a token within group g; that token lives on index chosen[g, e, c] // 16 of the expert axis. One list names no token twice. Among the first 32 slots of a list no two tokens live on the same index of the expert axis, nor among the last 32; so one expert takes at most 2 tokens of one device, and some device gives 2 to an expert in every list. Slots at or beyond counts[g, e] are ignored. `counts`: in every group some expert has all its slots valid.
All inputs are finite; a program needn't handle non-finite values.
Results may differ from a plain program's by a relative error of at most 0.028.
Values may be sent and summed in bfloat16 or wider, within the bound.
A program may use at most 64 MiB of HBM per device.

v0:
```python
import jax
import jax.numpy as jnp
from jax import lax
from jax.sharding import PartitionSpec as P

root_two_over_pi = 0.7978845608028654
cubic_coef = 0.044715


def partner(x, axis, apart):
    return lax.ppermute(x, axis, [(i, i ^ 1 << apart) for i in range(lax.axis_size(axis))])


def gelu_pair(pre_act):
    inner_arg = root_two_over_pi * (pre_act + cubic_coef * pre_act * pre_act * pre_act)
    tangent = jnp.tanh(inner_arg)
    act_value = 0.5 * pre_act * (1.0 + tangent)
    act_slope = 0.5 * (1.0 + tangent) + 0.5 * pre_act * (
        1.0 - tangent * tangent
    ) * root_two_over_pi * (1.0 + 3.0 * cubic_coef * pre_act * pre_act)
    return (act_value, act_slope)


def on_device(tokens_in, out_grad, chosen, counts, gates, w_up, w_down):
    tok_local = tokens_in.shape[0]
    width = tokens_in.shape[1]
    owners = lax.axis_size("expert")
    groups = lax.axis_size("dp")
    capacity = chosen.shape[2]
    half_cap = capacity // 2
    num_experts = chosen.shape[1]
    device = lax.axis_index("expert")
    expert = device // 2
    parity = device % 2
    highest = lax.Precision.HIGHEST
    my_lists = chosen[0]
    slot_ids = jnp.arange(capacity, dtype=jnp.int32)
    is_valid = slot_ids[None, :] < counts[0][:, None]
    owner_of = my_lists // tok_local
    local_of = my_lists % tok_local
    mine = jnp.logical_and(owner_of == device, is_valid)
    local_ids = jnp.arange(tok_local, dtype=jnp.int32)
    hits = jnp.logical_and(mine[:, :, None], local_of[:, :, None] == local_ids[None, None, :])
    picked = jnp.sum(hits.astype(jnp.float32).reshape(num_experts, 2, half_cap, tok_local), axis=2)
    picked_low = picked.astype(jnp.bfloat16)
    list_row = lax.dynamic_index_in_dim(my_lists, expert, 0, keepdims=False)
    count_here = lax.dynamic_index_in_dim(counts[0], expert, 0, keepdims=False)
    valid_here = slot_ids < count_here
    gate_here = jnp.where(
        valid_here,
        lax.dynamic_index_in_dim(gates[0], expert, 0, keepdims=False),
        jnp.zeros((), jnp.bfloat16),
    )
    owner_ids = jnp.arange(owners, dtype=jnp.int32)
    slot_map = jnp.logical_and(
        (list_row // tok_local)[:, None] == owner_ids[None, :], valid_here[:, None]
    )
    slot_map = slot_map.astype(jnp.float32).reshape(2, half_cap, owners)
    map_low = slot_map.astype(jnp.bfloat16)
    gate_rows = gate_here.reshape(2, half_cap)
    send_x = jnp.einsum(
        "erl,ld->red", picked_low, tokens_in, preferred_element_type=jnp.float32
    ).astype(jnp.bfloat16)
    send_g = jnp.einsum(
        "erl,ld->red", picked_low, out_grad, preferred_element_type=jnp.float32
    ).astype(jnp.bfloat16)
    send_x = jnp.repeat(send_x, 2, axis=1)
    send_g = jnp.repeat(send_g, 2, axis=1)
    recv_x, recv_g = (
        lax.all_to_all(send_x, "expert", split_axis=1, concat_axis=1, tiled=True),
        lax.all_to_all(send_g, "expert", split_axis=1, concat_axis=1, tiled=True),
    )
    rows_x = jnp.einsum("rij,rjd->rid", map_low, recv_x, preferred_element_type=jnp.float32).astype(
        jnp.bfloat16
    )
    rows_g = jnp.einsum("rij,rjd->rid", map_low, recv_g, preferred_element_type=jnp.float32).astype(
        jnp.bfloat16
    )
    all_x, all_g, all_gate = (
        lax.all_gather(rows_x, "dp", axis=1, tiled=True),
        lax.all_gather(rows_g, "dp", axis=1, tiled=True),
        lax.all_gather(gate_rows, "dp", axis=1, tiled=True),
    )
    flat_x = all_x.reshape(-1, width)
    flat_g = all_g.reshape(-1, width)
    flat_gate = all_gate.reshape(-1).astype(jnp.float32)
    up_part = w_up[0]
    down_part = w_down[0]
    pre_act = jnp.dot(flat_x, up_part, preferred_element_type=jnp.float32)
    act_value, act_slope = gelu_pair(pre_act)
    hidden = act_value.astype(jnp.bfloat16)
    back_grad = lax.dot_general(
        flat_g, down_part, (((1,), (1,)), ((), ())), preferred_element_type=jnp.float32
    )
    gate_terms = jnp.sum(hidden.astype(jnp.float32) * back_grad, axis=1)
    scaled = (flat_gate[:, None] * flat_g.astype(jnp.float32)).astype(jnp.bfloat16)
    pre_grad = (flat_gate[:, None] * back_grad * act_slope).astype(jnp.bfloat16)
    grad_down = lax.dot_general(
        hidden, scaled, (((0,), (0,)), ((), ())), preferred_element_type=jnp.float32
    )
    grad_up = lax.dot_general(
        flat_x, pre_grad, (((0,), (0,)), ((), ())), preferred_element_type=jnp.float32
    )
    dx_terms = lax.dot_general(
        pre_grad, up_part, (((1,), (1,)), ((), ())), preferred_element_type=jnp.float32
    )
    hidden_sum, gate_sums = (
        lax.psum_scatter(
            dx_terms.reshape(2, groups * half_cap, width).astype(jnp.bfloat16),
            "dp",
            scatter_dimension=1,
            tiled=True,
        ).astype(jnp.float32),
        lax.psum_scatter(
            gate_terms.reshape(2, groups * half_cap).astype(jnp.bfloat16),
            "dp",
            scatter_dimension=1,
            tiled=True,
        ).astype(jnp.float32),
    )
    spread = jnp.einsum("rij,rid->rjd", slot_map, hidden_sum, precision=highest)
    returned = lax.all_to_all(
        spread.astype(jnp.bfloat16), "expert", split_axis=1, concat_axis=1, tiled=True
    ).astype(spread.dtype)
    take_back = jnp.repeat(picked, 2, axis=0)
    in_grad = jnp.einsum("krl,rkd->ld", take_back, returned, precision=highest)
    partner_gate = partner(gate_sums, "expert", 0)
    gate_total = gate_sums + partner_gate
    gate_out = lax.dynamic_index_in_dim(gate_total, parity, 0, keepdims=False).reshape(
        1, 1, half_cap
    )
    return (
        in_grad.astype(jnp.bfloat16),
        grad_up.astype(jnp.bfloat16)[None],
        grad_down.astype(jnp.bfloat16)[None],
        gate_out,
    )


def solution(mesh):
    placed = (
        P(("dp", "expert"), None),
        P(("dp", "expert"), None),
        P("dp", None, None),
        P("dp", None),
        P("dp", None, None),
        P("expert", None, "dp"),
        P("expert", "dp", None),
    )
    return jax.shard_map(
        on_device,
        mesh=mesh,
        in_specs=placed,
        out_specs=(
            P(("dp", "expert"), None),
            P("expert", None, "dp"),
            P("expert", "dp", None),
            P("dp", "expert", None),
        ),
        check_vma=False,
    )
```

profile of v0, /device:TPU:0, one launch (start us, length us, event | category | flops | bytes accessed | tf_op | source)
XLA Modules:
  0.0 65.2 jit_solution(9272128698797933885)
XLA Ops:
  0.7 0.8 %squeeze.25 = s32[16,2,32]{2,1,0:T(2,128)S(1)} reshape(s32[1,16,64]{2,1,0:T(8,128)} %param.9) | data formatting | bytes 8192 | tf_op jit(solution)/shard_map/squeeze | solution.py:36
  1.5 0.7 %compare_and_fusion = pred[16,2,32]{2,1,0:T(4,128)(4,1)S(1)} fusion(s32[16,2,32]{2,1,0:T(2,128)S(1)} %squeeze.25, s32[2,32]{1,0:T(2,128)S(1)} %multiply_add_fusion.1, s32[]{:T(128)S(6)} %axis_index.12, s32[16]{0:T(128)} %bitcast.60), kind=kLoop, calls=%fused_computation.43 | loop fusion | flops 18432 | bytes 5444 | tf_op jit(solution)/shard_map/and | solution.py:41
  2.7 0.9 %broadcast_in_dim.31 = bf16[2,16,2,2048]{3,0,2,1:T(2,128)(2,1)} broadcast(bf16[2,16,2048]{2,0,1:T(2,128)(2,1)S(1)} %copy.28), dimensions={0,1,3} | broadcast | bytes 393216 | tf_op jit(solution)/shard_map/broadcast_in_dim | solution.py:67
  3.6 7.3 %all-to-all-start.1 = ((bf16[2,32,2048]{2,0,1:T(2,128)(2,1)}), bf16[2,32,2048]{2,0,1:T(2,128)(2,1)S(1)}, u32[]{:S(2)}, u32[]{:S(2)}) async-start(bf16[2,32,2048]{2,0,1:T(2,128)(2,1)} %bitcast.11), calls=%async_computation.1 | async-start | bytes 524288 | tf_op jit(solution)/shard_map/all_to_all | solution.py:70
  10.9 1.0 %fusion.9 = bf16[2,16,2048]{2,1,0:T(8,128)(2,1)S(1)} fusion(bf16[16,2048]{1,0:T(8,128)(2,1)} %param.8, bf16[16,2,16]{2,1,0:T(2,128)(2,1)S(1)} %convert_element_type.85), kind=kOutput, calls=%fused_computation.14 | convolution fusion | flops 2162688 | bytes 197632 | tf_op jit(solution)/shard_map/erl,ld->red/dot_general | solution.py:64
  11.9 1.2 %constant_dynamic-slice_fusion.2 = s32[1,1]{1,0:T(1,128)} fusion(s32[1,16]{1,0:T(1,128)} %param.10, s32[]{:T(128)S(6)} %select_n.64), kind=kLoop, calls=%fused_computation.66 | loop fusion | bytes 12 | tf_op jit(solution)/shard_map/jit(dynamic_index_in_dim)/dynamic_slice | solution.py:47
  13.2 0.7 %fusion.36 = s32[64]{0:T(128)S(1)} fusion(s32[1,16,64]{2,1,0:T(8,128)} %param.9, s32[]{:T(128)S(6)} %select_n.64), kind=kLoop, calls=%fused_computation.68 | loop fusion | bytes 516 | tf_op jit(solution)/shard_map/jit(dynamic_index_in_dim)/dynamic_slice | solution.py:46
  14.1 0.7 %broadcast_compare_fusion.2 = pred[2,32]{1,0:T(4,128)(4,1)S(1)} fusion(s32[]{:T(128)} %bitcast.2), kind=kLoop, calls=%fused_computation.72 | loop fusion | flops 192 | bytes 68 | tf_op jit(solution)/shard_map/lt | solution.py:48
  14.8 1.3 %fusion.39 = f32[64]{0:T(128)S(1)} fusion(bf16[1,16,64]{2,1,0:T(8,128)(2,1)} %param.11, s32[]{:T(128)S(6)} %select_n.64, s32[]{:T(128)} %bitcast.2), kind=kLoop, calls=%fused_computation.73 | loop fusion | flops 192 | bytes 392 | tf_op jit(solution)/shard_map/convert_element_type | solution.py:86
  16.1 5.4 %all-to-all-done.1 = bf16[2,32,2048]{2,0,1:T(2,128)(2,1)S(1)} async-done(((bf16[2,32,2048]{2,0,1:T(2,128)(2,1)}), bf16[2,32,2048]{2,0,1:T(2,128)(2,1)S(1)}, u32[]{:S(2)}, u32[]{:S(2)}) %all-to-all-start.1) | async-done | bytes 262176 | tf_op jit(solution)/shard_map/all_to_all | solution.py:70
  21.5 0.9 %broadcast_in_dim.30 = bf16[2,16,2,2048]{3,0,2,1:T(2,128)(2,1)} broadcast(bf16[2,16,2048]{2,0,1:T(2,128)(2,1)S(1)} %copy.24), dimensions={0,1,3} | broadcast | bytes 393216 | tf_op jit(solution)/shard_map/broadcast_in_dim | solution.py:68
  22.3 2.6 %all-to-all-start = ((bf16[2,32,2048]{2,0,1:T(2,128)(2,1)}), bf16[2,32,2048]{2,0,1:T(2,128)(2,1)S(1)}, u32[]{:S(2)}, u32[]{:S(2)}) async-start(bf16[2,32,2048]{2,0,1:T(2,128)(2,1)} %bitcast.6), calls=%async_computation | async-start | bytes 524288 | tf_op jit(solution)/shard_map/all_to_all | solution.py:71
  24.9 0.3 convolution_convert_fusion.1
  25.2 4.9 %fusion.2 = f32[64,2048]{1,0:T(8,128)S(1)} fusion(bf16[64,2048]{1,0:T(8,128)(2,1)S(1)} %bitcast.54, bf16[1,2048,2048]{2,1,0:T(8,128)(2,1)} %param.12), kind=kOutput, calls=%fused_computation.2 | convolution fusion | flops 536870912 | bytes 9175040 | tf_op jit(solution)/shard_map/dot_general | solution.py:89
  30.2 5.3 %all-to-all-done = bf16[2,32,2048]{2,0,1:T(2,128)(2,1)S(1)} async-done(((bf16[2,32,2048]{2,0,1:T(2,128)(2,1)}), bf16[2,32,2048]{2,0,1:T(2,128)(2,1)S(1)}, u32[]{:S(2)}, u32[]{:S(2)}) %all-to-all-start) | async-done | bytes 262176 | tf_op jit(solution)/shard_map/all_to_all | solution.py:71
  35.5 0.3 convolution_convert_fusion.2
  35.8 6.2 %multiply_reduce_fusion = (bf16[64]{0:T(256)(128)(2,1)S(1)}, bf16[64,2048]{1,0:T(8,128)(2,1)S(1)}) fusion(f32[64,2048]{1,0:T(8,128)S(1)} %fusion.2, f32[64]{0:T(128)S(1)} %fusion.39, bf16[64,2048]{1,0:T(8,128)(2,1)S(1)} %bitcast.57, bf16[1,2048,2048]{2,1,0:T(8,128)(2,1)} %param.13), kind=kOutput, calls=%fused_computation.27 | convolution fusion | flops 540147648 | bytes 9437568 | tf_op jit(solution)/shard_map/dot_general | solution.py:92
  42.2 6.0 %fusion.6 = bf16[2,32,2048]{2,1,0:T(8,128)(2,1)S(1)} fusion(bf16[2,32,2048]{2,1,0:T(8,128)(2,1)S(1)} %bitcast.56, bf16[1,2048,2048]{2,1,0:T(8,128)(2,1)} %param.12), kind=kOutput, calls=%fused_computation.11 | convolution fusion | flops 537001984 | bytes 8912896 | tf_op jit(solution)/shard_map/dot_general | solution.py:104
  48.4 1.0 %copy.31 = bf16[2,32,2048]{2,0,1:T(2,128)(2,1)} copy(bf16[2,32,2048]{2,1,0:T(8,128)(2,1)S(1)} %convolution_convert_fusion) | data formatting | bytes 524288 | tf_op jit(solution)/shard_map/convert_element_type | solution.py:123
  49.4 2.8 %all-to-all-start.2 = ((bf16[2,32,2048]{2,0,1:T(2,128)(2,1)}), bf16[2,32,2048]{2,0,1:T(2,128)(2,1)S(1)}, u32[]{:S(2)}, u32[]{:S(2)}) async-start(bf16[2,32,2048]{2,0,1:T(2,128)(2,1)} %copy.31), calls=%async_computation.2 | async-start | bytes 524288 | tf_op jit(solution)/shard_map/all_to_all | solution.py:122
  52.2 5.8 %convert_bitcast_fusion = bf16[1,2048,2048]{2,1,0:T(8,128)(2,1)} fusion(bf16[64,2048]{1,0:T(8,128)(2,1)S(1)} %bitcast.58, f32[64]{0:T(128)S(1)} %fusion.39, f32[64,2048]{1,0:T(8,128)S(1)} %fusion.2), kind=kOutput, calls=%fused_computation.6 | convolution fusion | flops 542638080 | bytes 9175296 | tf_op jit(solution)/shard_map/dot_general | solution.py:98
  58.0 5.8 %convert_bitcast_fusion.1 = bf16[1,2048,2048]{2,1,0:T(8,128)(2,1)} fusion(bf16[64,2048]{1,0:T(8,128)(2,1)S(1)} %bitcast.55, bf16[64,2048]{1,0:T(8,128)(2,1)S(1)} %get-tuple-element.5), kind=kOutput, calls=%fused_computation.7 | convolution fusion | flops 541065216 | bytes 8912896 | tf_op jit(solution)/shard_map/dot_general | solution.py:101
  63.7 0.5 fusion.38
  64.3 0.9 %fusion.11 = bf16[16,2048]{1,0:T(8,128)(2,1)} fusion(f32[32,2,16]{2,0,1:T(8,128)S(1)} %bitcast.59, bf16[2,32,2048]{2,0,1:T(2,128)(2,1)S(1)} %all-to-all-done.2), kind=kOutput, calls=%fused_computation.17 | convolution fusion | flops 25198592 | bytes 331776 | tf_op jit(solution)/shard_map/krl,rkd->ld/dot_general | solution.py:126
  (19 shorter events, 1.1 us)
Async XLA Ops:
  0.6 1.8 %copy-start = (bf16[16,2048]{1,0:T(8,128)(2,1)S(1)}, bf16[16,2048]{1,0:T(8,128)(2,1)}, u32[]{:S(2)}) copy-start(bf16[16,2048]{1,0:T(8,128)(2,1)} %param.7) | copy-start | bytes 196612
  3.6 17.9 %all-to-all-start.1 = ((bf16[2,32,2048]{2,0,1:T(2,128)(2,1)}), bf16[2,32,2048]{2,0,1:T(2,128)(2,1)S(1)}, u32[]{:S(2)}, u32[]{:S(2)}) async-start(bf16[2,32,2048]{2,0,1:T(2,128)(2,1)} %bitcast.11), calls=%async_computation.1 | async-start | bytes 524288 | tf_op jit(solution)/shard_map/all_to_all | solution.py:70
  22.3 13.2 %all-to-all-start = ((bf16[2,32,2048]{2,0,1:T(2,128)(2,1)}), bf16[2,32,2048]{2,0,1:T(2,128)(2,1)S(1)}, u32[]{:S(2)}, u32[]{:S(2)}) async-start(bf16[2,32,2048]{2,0,1:T(2,128)(2,1)} %bitcast.6), calls=%async_computation | async-start | bytes 524288 | tf_op jit(solution)/shard_map/all_to_all | solution.py:71
  42.2 21.6 %collective-permute-start = (f32[2,32]{1,0:T(2,128)S(1)}, f32[2,32]{1,0:T(2,128)S(1)}, u32[]{:S(2)}, u32[]{:S(2)}) collective-permute-start(f32[2,32]{1,0:T(2,128)S(1)} %reshape.197), channel_id=1, source_target_pairs={{0,1},{1,0},{2,3},{3,2},{4,5},{5,4},{6,7},{7,6},{8,9},{9,8},{10,11... | collective-permute-start | bytes 776 | tf_op jit(solution)/shard_map/ppermute | solution.py:11
  49.4 14.9 %all-to-all-start.2 = ((bf16[2,32,2048]{2,0,1:T(2,128)(2,1)}), bf16[2,32,2048]{2,0,1:T(2,128)(2,1)S(1)}, u32[]{:S(2)}, u32[]{:S(2)}) async-start(bf16[2,32,2048]{2,0,1:T(2,128)(2,1)} %copy.31), calls=%async_computation.2 | async-start | bytes 524288 | tf_op jit(solution)/shard_map/all_to_all | solution.py:122
where the time goes:
time: 65.8 us; the launch traced here: 65.2 us
  matrix products  31.7 us (48%)
  starting transfers between devices  12.6 us (19%)
  waiting for transfers between devices  10.7 us (16%)
  local copies, waits for them, and re-layouts  6.39 us (10%)
  other arithmetic  2.96 us (4%)
  between operations  0.82 us (1%)
    all_to_all x1, starting transfers between devices, on_device(): lax.all_to_all(send_x, 'expert', split_axis=1, concat_axis=1, tiled=True)  7.29 us
    dot_general x1, matrix products, on_device(): lax.dot_general(flat_g, down_part, (((1,), (1,)), ((), ())), preferred_el...  6.23 us
    dot_general x1, matrix products, on_device(): lax.dot_general(pre_grad, up_part, (((1,), (1,)), ((), ())), preferred_el...  6.04 us
    dot_general x1, matrix products, on_device(): lax.dot_general(hidden, scaled, (((0,), (0,)), ((), ())), preferred_eleme...  5.81 us
    dot_general x1, matrix products, on_device(): lax.dot_general(flat_x, pre_grad, (((0,), (0,)), ((), ())), preferred_ele...  5.77 us
    all_to_all x1, waiting for transfers between devices, on_device(): lax.all_to_all(send_x, 'expert', split_axis=1, concat_axis=1, tiled=True)  5.38 us
    all_to_all x1, waiting for transfers between devices, on_device(): lax.all_to_all(send_g, 'expert', split_axis=1, concat_axis=1, tiled=True)  5.35 us
    dot_general x1, matrix products, on_device(): pre_act = jnp.dot(flat_x, up_part, preferred_element_type=jnp.float32)  4.95 us
  transfers between devices with their start and end apart: 4, of which 2 were waited for; matrix products, arithmetic and copies ran while one was open for 46% of the time, Pallas kernels for 0%

commit v1 on v0

--- a/solution.py
+++ b/solution.py
@@ -1,6 +1,9 @@
+import functools
 import jax
 import jax.numpy as jnp
 from jax import lax
+from jax.experimental import pallas as pl
+from jax.experimental.pallas import tpu as pltpu
 from jax.sharding import PartitionSpec as P
 
 root_two_over_pi = 0.7978845608028654
@@ -21,7 +24,7 @@
     return (act_value, act_slope)
 
 
-def on_device(tokens_in, out_grad, chosen, counts, gates, w_up, w_down):
+def on_device_any(tokens_in, out_grad, chosen, counts, gates, w_up, w_down):
     tok_local = tokens_in.shape[0]
     width = tokens_in.shape[1]
     owners = lax.axis_size("expert")
@@ -137,6 +140,384 @@
     )
 
 
+NB = 8
+HOP = 2 * NB
+
+
+def is_one(cond):
+    return jnp.where(cond, 1.0, 0.0)
+
+
+def iota(shape, dim):
+    return lax.broadcasted_iota(jnp.int32, shape, dim)
+
+
+def f32_dot(a, b, dims=((1,), (0,))):
+    return lax.dot_general(a, b, (dims, ((), ())), preferred_element_type=jnp.float32)
+
+
+def expert_kernel(
+    x_ref, g_ref, chosen_ref, counts_ref, gates_ref, up_hbm, down_hbm,
+    in_grad_ref, gate_ref, rows_ref, scaled_ref, hidden_ref, pg_ref,
+    up_v, down_v, send, recv, grows, slope, dx_acc, dx_out, dx_in, gate_out, gate_in,
+    ret_send, ret_recv,
+    w_sem, send_sem, recv_sem, fwd_send, fwd_recv, ret_ssem, ret_rsem, pair_send, pair_recv,
+):
+    tok, width = x_ref.shape
+    experts, cap = chosen_ref.shape[1:]
+    ff = up_v.shape[1]
+    half = cap // 2
+    wide = width // NB
+    rows = 2 * experts
+    log_tok = tok.bit_length() - 1
+    me = lax.axis_index("expert")
+    chip = me // 2
+    core = me % 2
+    mate = me + 1 - 2 * core
+
+    up_copy = pltpu.make_async_copy(up_hbm.at[0], up_v, w_sem.at[0])
+    down_copy = pltpu.make_async_copy(down_hbm.at[0], down_v, w_sem.at[1])
+    up_copy.start()
+    down_copy.start()
+
+    def far(k):
+        return lax.rem(chip + k, experts)
+
+    barrier = pltpu.get_barrier_semaphore()
+    pl.semaphore_signal(barrier, inc=1, device_id={"expert": mate})
+
+    def greet(k, _):
+        pl.semaphore_signal(barrier, inc=1, device_id={"expert": 2 * far(k) + core})
+        return 0
+
+    lax.fori_loop(1, experts, greet, 0)
+
+    chosen = chosen_ref[0]
+    slot = iota((experts, cap), 1)
+    counts = counts_ref[...].astype(jnp.float32)
+    diag = iota((experts, experts), 0) == iota((experts, experts), 1)
+    count_col = jnp.sum(jnp.where(diag, counts, 0.0), axis=1, keepdims=True)
+    local = chosen - me * tok
+    mine = (local >= 0) & (local < tok) & (slot.astype(jnp.float32) < count_col)
+    local_one = local.astype(jnp.float32) + 1.0
+    lanes = NB * tok
+    named = jnp.concatenate(
+        [
+            jnp.broadcast_to(
+                jnp.sum(
+                    jnp.where(mine & ((slot >= half) == bool(r)), local_one, 0.0),
+                    axis=1, keepdims=True,
+                ),
+                (experts, lanes),
+            )
+            for r in range(2)
+        ],
+        axis=0,
+    ).astype(jnp.bfloat16)
+    tall = experts * HOP
+    ti, tc = iota((tall, rows), 0), iota((tall, rows), 1)
+    want = (ti & (HOP - 1)) // NB * experts + ti // HOP
+    spread = is_one(want == tc).astype(jnp.bfloat16)
+    full = f32_dot(spread, named)
+    qi, ql = iota((tall, lanes), 0), iota((tall, lanes), 1)
+    pick = is_one(
+        (full == ((ql & (tok - 1)) + 1).astype(jnp.float32))
+        & ((qi & (NB - 1)) == (ql >> log_tok))
+    ).astype(jnp.bfloat16)
+
+    pl.semaphore_wait(barrier, experts)
+
+    for a, ref in enumerate((x_ref, g_ref)):
+        stacked = jnp.concatenate(
+            [ref[:, j * wide:(j + 1) * wide] for j in range(NB)], axis=0
+        )
+        packed = f32_dot(pick, stacked).astype(jnp.bfloat16)
+        send[a] = packed.reshape(experts, HOP, wide)
+
+        def push(k, _, a=a):
+            dst = far(experts - k)
+            pltpu.make_async_remote_copy(
+                src_ref=send.at[a, dst],
+                dst_ref=recv.at[a, core, chip],
+                send_sem=send_sem.at[a, dst],
+                recv_sem=recv_sem.at[a, chip],
+                device_id={"expert": 2 * dst + core},
+            ).start()
+            return 0
+
+        lax.fori_loop(1, experts, push, 0)
+        recv[a, core, chip] = send[a, chip]
+
+    pi, pc = iota((tall, tall), 0), iota((tall, tall), 1)
+    unpack = is_one(
+        pc == ((pi & (rows - 1)) >> 1) * HOP + (pi & 1) * NB + pi // rows
+    ).astype(jnp.bfloat16)
+
+    def arrive(a):
+        def one(k, _):
+            src = far(k)
+            pltpu.make_async_remote_copy(
+                src_ref=send.at[a, src],
+                dst_ref=recv.at[a, core, src],
+                send_sem=send_sem.at[a, src],
+                recv_sem=recv_sem.at[a, src],
+                device_id={"expert": 2 * src + core},
+            ).wait()
+            return 0
+
+        lax.fori_loop(1, experts, one, 0)
+        copy = pltpu.make_async_remote_copy(
+            src_ref=recv.at[a, core],
+            dst_ref=recv.at[a, core],
+            send_sem=fwd_send.at[a],
+            recv_sem=fwd_recv.at[a],
+            device_id={"expert": mate},
+        )
+        copy.start()
+        return copy
+
+    def unfold(a, parity, out):
+        flat = f32_dot(unpack, recv[a, parity].reshape(tall, wide)).astype(jnp.bfloat16)
+        at = pl.ds(pl.multiple_of(parity * rows, rows), rows)
+        for j in range(NB):
+            out[at, j * wide:(j + 1) * wide] = flat[j * rows:(j + 1) * rows]
+
+    def other_half(a):
+        return pltpu.make_async_remote_copy(
+            src_ref=recv.at[a, 1 - core],
+            dst_ref=recv.at[a, 1 - core],
+            send_sem=fwd_send.at[a],
+            recv_sem=fwd_recv.at[a],
+            device_id={"expert": mate},
+        )
+
+    my_list = chosen_ref[0, pl.ds(chip, 1), :]
+    my_gate = gates_ref[0].astype(jnp.float32)
+    my_gate = jnp.sum(
+        jnp.where(iota((experts, cap), 0) == chip, my_gate, 0.0), axis=0, keepdims=True
+    )
+    my_count = jnp.sum(
+        jnp.where(iota((1, experts), 1) == chip, counts, 0.0), axis=1, keepdims=True
+    )
+    owner = my_list >> log_tok
+    late = jnp.where(iota((1, cap), 1) >= half, 1, 0)
+    place = (owner & 1) * rows + (owner >> 1) * 2 + late
+    live = iota((1, cap), 1).astype(jnp.float32) < my_count
+    seat = is_one((iota((2 * rows, cap), 0) == place) & live)
+    weight = jnp.sum(seat * my_gate, axis=1, keepdims=True)
+
+    fwd_x = arrive(0)
+    unfold(0, core, rows_ref)
+    up_copy.wait()
+    other_half(0).wait_recv()
+    unfold(0, 1 - core, rows_ref)
+
+    step = 512
+    x_rows = rows_ref[...]
+
+    def forward(c, _):
+        cols = pl.ds(pl.multiple_of(c * step, step), step)
+        value, tilt = gelu_pair(f32_dot(x_rows, up_v[:, cols]))
+        hidden_ref[:, cols] = value.astype(jnp.bfloat16)
+        slope[:, cols] = tilt
+        return 0
+
+    lax.fori_loop(0, ff // step, forward, 0)
+
+    fwd_g = arrive(1)
+    unfold(1, core, grows)
+    down_copy.wait()
+    other_half(1).wait_recv()
+    unfold(1, 1 - core, grows)
+    g_rows = grows[...]
+    scaled_ref[...] = (weight * g_rows.astype(jnp.float32)).astype(jnp.bfloat16)
+    dx_acc[...] = jnp.zeros_like(dx_acc)
+
+    def backward(c, total):
+        cols = pl.ds(pl.multiple_of(c * step, step), step)
+        back = f32_dot(g_rows, down_v[cols, :], ((1,), (1,)))
+        pre_grad = (weight * back * slope[:, cols]).astype(jnp.bfloat16)
+        pg_ref[:, cols] = pre_grad
+        dx_acc[...] += f32_dot(pre_grad, up_v[:, cols], ((1,), (1,)))
+        return total + jnp.sum(
+            hidden_ref[:, cols].astype(jnp.float32) * back, axis=1, keepdims=True
+        )
+
+    gate_terms = lax.fori_loop(
+        0, ff // step, backward, jnp.zeros((2 * rows, 1), jnp.float32)
+    )
+
+    theirs = pl.ds(pl.multiple_of((1 - core) * rows, rows), rows)
+    ours = pl.ds(pl.multiple_of(core * rows, rows), rows)
+    dx_out[...] = dx_acc[theirs, :].astype(jnp.bfloat16)
+    dx_copy = pltpu.make_async_remote_copy(
+        src_ref=dx_out, dst_ref=dx_in,
+        send_sem=pair_send.at[0], recv_sem=pair_recv.at[0], device_id={"expert": mate},
+    )
+    dx_copy.start()
+    low = gate_terms.astype(jnp.bfloat16).astype(jnp.float32)
+    by_slot = jnp.sum(seat * low, axis=0, keepdims=True)
+    gate_out[...] = jnp.broadcast_to(
+        jnp.concatenate([by_slot, jnp.zeros((1, 128 - cap), jnp.float32)], axis=1), (8, 128)
+    )
+    gate_copy = pltpu.make_async_remote_copy(
+        src_ref=gate_out, dst_ref=gate_in,
+        send_sem=pair_send.at[1], recv_sem=pair_recv.at[1], device_id={"expert": mate},
+    )
+    gate_copy.start()
+    dx_copy.wait()
+    both = (
+        dx_acc[ours, :].astype(jnp.bfloat16).astype(jnp.float32)
+        + dx_in[...].astype(jnp.float32)
+    ).astype(jnp.bfloat16)
+    stacked = jnp.concatenate([both[:, j * wide:(j + 1) * wide] for j in range(NB)], axis=0)
+    packed = f32_dot(unpack, stacked, ((0,), (0,))).astype(jnp.bfloat16)
+    ret_send[...] = packed.reshape(experts, HOP, wide)
+
+    def give_back(k, _):
+        dst = far(experts - k)
+        pltpu.make_async_remote_copy(
+            src_ref=ret_send.at[dst],
+            dst_ref=ret_recv.at[chip],
+            send_sem=ret_ssem.at[dst],
+            recv_sem=ret_rsem.at[chip],
+            device_id={"expert": 2 * dst + core},
+        ).start()
+        return 0
+
+    lax.fori_loop(1, experts, give_back, 0)
+    ret_recv[chip] = ret_send[chip]
+
+    gate_copy.wait()
+    total = gate_out[0:1, :cap] + gate_in[0:1, :cap]
+    gate_ref[0] = jnp.where(core == 0, total[:, :half], total[:, half:])
+    fwd_x.wait_send()
+    fwd_g.wait_send()
+
+    def taken(k, _):
+        src = far(k)
+        pltpu.make_async_remote_copy(
+            src_ref=ret_send.at[src],
+            dst_ref=ret_recv.at[src],
+            send_sem=ret_ssem.at[src],
+            recv_sem=ret_rsem.at[src],
+            device_id={"expert": 2 * src + core},
+        ).wait()
+        return 0
+
+    lax.fori_loop(1, experts, taken, 0)
+    folded = f32_dot(pick, ret_recv[...].reshape(tall, wide), ((0,), (0,))).astype(jnp.bfloat16)
+    for j in range(NB):
+        in_grad_ref[:, j * wide:(j + 1) * wide] = folded[j * tok:(j + 1) * tok]
+
+
+def grads_kernel(rows_ref, pg_ref, hidden_ref, scaled_ref, up_ref, down_ref):
+    up_ref[0] = f32_dot(rows_ref[...], pg_ref[...], ((0,), (0,))).astype(jnp.bfloat16)
+    down_ref[0] = f32_dot(hidden_ref[...], scaled_ref[...], ((0,), (0,))).astype(jnp.bfloat16)
+
+
+def on_device_pairs(tokens_in, out_grad, chosen, counts, gates, w_up, w_down):
+    tok, width = tokens_in.shape
+    experts, cap = chosen.shape[1:]
+    ff = w_up.shape[2]
+    rows = 2 * experts
+    wide = width // NB
+    bf16, f32 = jnp.bfloat16, jnp.float32
+    vmem = pl.BlockSpec(memory_space=pltpu.VMEM)
+    hbm = pl.BlockSpec(memory_space=pl.ANY)
+    dma = pltpu.SemaphoreType.DMA
+    in_grad, gate_grad, x_rows, scaled, hidden, pre_grad = pl.pallas_call(
+        expert_kernel,
+        out_shape=(
+            jax.ShapeDtypeStruct((tok, width), bf16),
+            jax.ShapeDtypeStruct((1, 1, cap // 2), f32),
+            jax.ShapeDtypeStruct((2 * rows, width), bf16),
+            jax.ShapeDtypeStruct((2 * rows, width), bf16),
+            jax.ShapeDtypeStruct((2 * rows, ff), bf16),
+            jax.ShapeDtypeStruct((2 * rows, ff), bf16),
+        ),
+        in_specs=[vmem] * 5 + [hbm] * 2,
+        out_specs=(vmem,) * 6,
+        scratch_shapes=[
+            pltpu.VMEM((width, ff), bf16),
+            pltpu.VMEM((ff, width), bf16),
+            pltpu.VMEM((2, experts, HOP, wide), bf16),
+            pltpu.VMEM((2, 2, experts, HOP, wide), bf16),
+            pltpu.VMEM((2 * rows, width), bf16),
+            pltpu.VMEM((2 * rows, ff), f32),
+            pltpu.VMEM((2 * rows, width), f32),
+            pltpu.VMEM((rows, width), bf16),
+            pltpu.VMEM((rows, width), bf16),
+            pltpu.VMEM((8, 128), f32),
+            pltpu.VMEM((8, 128), f32),
+            pltpu.VMEM((experts, HOP, wide), bf16),
+            pltpu.VMEM((experts, HOP, wide), bf16),
+            dma((2,)),
+            dma((2, experts)),
+            dma((2, experts)),
+            dma((2,)),
+            dma((2,)),
+            dma((experts,)),
+            dma((experts,)),
+            dma((2,)),
+            dma((2,)),
+        ],
+        compiler_params=pltpu.CompilerParams(
+            collective_id=0, has_side_effects=True, vmem_limit_bytes=40 << 20
+        ),
+        cost_estimate=pl.CostEstimate(
+            flops=6 * 2 * rows * width * ff,
+            bytes_accessed=4 * width * ff,
+            transcendentals=2 * rows * ff,
+        ),
+    )(tokens_in, out_grad, chosen, counts, gates, w_up, w_down)
+
+    steps = 8
+    grad_up, grad_down = pl.pallas_call(
+        grads_kernel,
+        grid=(steps,),
+        out_shape=(
+            jax.ShapeDtypeStruct((1, width, ff), bf16),
+            jax.ShapeDtypeStruct((1, ff, width), bf16),
+        ),
+        in_specs=[
+            pl.BlockSpec((2 * rows, width // steps), lambda i: (0, i)),
+            pl.BlockSpec((2 * rows, ff), lambda i: (0, 0)),
+            pl.BlockSpec((2 * rows, ff // steps), lambda i: (0, i)),
+            pl.BlockSpec((2 * rows, width), lambda i: (0, 0)),
+        ],
+        out_specs=(
+            pl.BlockSpec((1, width // steps, ff), lambda i: (0, i, 0)),
+            pl.BlockSpec((1, ff // steps, width), lambda i: (0, i, 0)),
+        ),
+        compiler_params=pltpu.CompilerParams(vmem_limit_bytes=32 << 20),
+        cost_estimate=pl.CostEstimate(
+            flops=8 * rows * width * ff,
+            bytes_accessed=4 * width * ff,
+            transcendentals=0,
+        ),
+    )(x_rows, pre_grad, hidden, scaled)
+    return in_grad, grad_up, grad_down, gate_grad
+
+
+def on_device(mesh, *args):
+    tok, width = args[0].shape
+    experts, cap = args[2].shape[1:]
+    two = lambda v: v & (v - 1) == 0
+    fits = (
+        mesh.shape["dp"] == 1
+        and mesh.shape["expert"] == 2 * experts
+        and cap == 4 * experts
+        and cap <= 128
+        and tok % 16 == 0
+        and width % 2048 == 0
+        and args[5].shape[2] % 2048 == 0
+        and two(tok)
+        and two(experts)
+    )
+    return (on_device_pairs if fits else on_device_any)(*args)
+
+
 def solution(mesh):
     placed = (
         P(("dp", "expert"), None),
@@ -148,7 +529,7 @@
         P("expert", "dp", None),
     )
     return jax.shard_map(
-        on_device,
+        functools.partial(on_device, mesh),
         mesh=mesh,
         in_specs=placed,
         out_specs=(

time: 65.8 us -> 50.5 us (0.77)
  Pallas kernels: 0 us -> 41.3 us
  matrix products: 31.7 us -> 0 us
  starting transfers between devices: 12.6 us -> 0 us
  waiting for transfers between devices: 10.7 us -> 0 us
  other arithmetic: 2.96 us -> 0 us
  local copies, waits for them, and re-layouts: 6.39 us -> 8.23 us
    pallas_call x0 -> x2, Pallas kernels: none -> 41.3 us  [the longest x1 33.5 us: on_device_pairs(): pl.pallas_call(expert_kernel, out_shape=(jax.ShapeDtypeStruct((tok, width...]
    dot_general x11 -> x0, matrix products: 31.7 us -> none  [the longest x1 6.23 us: on_device(): lax.dot_general(flat_g, down_part, (((1,), (1,)), ((), ())), preferred_el...]
    all_to_all x3 -> x0, starting transfers between devices: 12.6 us -> none  [the longest x1 7.29 us: on_device(): lax.all_to_all(send_x, 'expert', split_axis=1, concat_axis=1, tiled=True)]
    all_to_all x3 -> x0, waiting for transfers between devices: 10.7 us -> none  [the longest x1 5.38 us: on_device(): lax.all_to_all(send_x, 'expert', split_axis=1, concat_axis=1, tiled=True)]
    unnamed x2 -> x14, local copies, waits for them, and re-layouts: 0.01 us -> 8.23 us
    dynamic_slice x2 -> x0, local copies, waits for them, and re-layouts: 1.95 us -> none  [the longest x1 1.24 us: on_device(): count_here = lax.dynamic_index_in_dim(counts[0], expert, 0, keepdims=False)]
    broadcast_in_dim x3 -> x0, local copies, waits for them, and re-layouts: 1.73 us -> none  [the longest x1 0.86 us: on_device(): send_x = jnp.repeat(send_x, 2, axis=1)]
    convert_element_type x2 -> x0, other arithmetic: 1.35 us -> none  [the longest x1 1.34 us: on_device(): flat_gate = all_gate.reshape(-1).astype(jnp.float32)]
  transfers between devices with their start and end apart: 4 -> 0, of which waited for: 2 -> 0; matrix products, arithmetic and copies ran while one was open for 46% -> 0% of each run, Pallas kernels for 0% -> 0%
where the time goes in v1:
time: 50.5 us; the launch traced here: 50.2 us
  Pallas kernels  41.3 us (82%)
  local copies, waits for them, and re-layouts  8.23 us (16%)
  between operations  0.66 us (1%)
    pallas_call x1, Pallas kernels, on_device_pairs(): pl.pallas_call(expert_kernel, out_shape=(jax.ShapeDtypeStruct((tok, width...  33.5 us
    unnamed x14, local copies, waits for them, and re-layouts  8.23 us
    pallas_call x1, Pallas kernels, on_device_pairs(): pl.pallas_call(grads_kernel, grid=(steps,), out_shape=(jax.ShapeDtypeStru...  7.83 us

profile of v1, /device:TPU:0, one launch (start us, length us, event | category | flops | bytes accessed | tf_op | source)
XLA Modules:
  0.0 50.2 jit_solution(10336087613329955461)
XLA Ops:
  0.6 0.0 copy-start
  0.6 3.4 %copy-done = bf16[1,2048,2048]{2,1,0:T(8,128)(2,1)S(1)} copy-done((bf16[1,2048,2048]{2,1,0:T(8,128)(2,1)S(1)}, bf16[1,2048,2048]{2,1,0:T(8,128)(2,1)}, u32[]{:S(2)}) %copy-start) | copy-done | bytes 8388632
  4.0 0.0 copy-start.1
  4.0 0.8 %copy-done.1 = bf16[16,2048]{1,0:T(8,128)(2,1)S(1)} copy-done((bf16[16,2048]{1,0:T(8,128)(2,1)S(1)}, bf16[16,2048]{1,0:T(8,128)(2,1)}, u32[]{:S(2)}) %copy-start.1) | copy-done | bytes 65560
  4.9 0.0 copy-start.2
  4.9 0.8 %copy-done.2 = bf16[16,2048]{1,0:T(8,128)(2,1)S(1)} copy-done((bf16[16,2048]{1,0:T(8,128)(2,1)S(1)}, bf16[16,2048]{1,0:T(8,128)(2,1)}, u32[]{:S(2)}) %copy-start.2) | copy-done | bytes 65560
  5.7 0.0 copy-start.3
  5.7 0.7 %copy-done.3 = s32[1,16,64]{2,1,0:T(8,128)S(1)} copy-done((s32[1,16,64]{2,1,0:T(8,128)S(1)}, s32[1,16,64]{2,1,0:T(8,128)}, u32[]{:S(2)}) %copy-start.3) | copy-done | bytes 4120
  6.4 0.0 copy-start.4
  6.4 0.7 %copy-done.4 = bf16[1,16,64]{2,1,0:T(8,128)(2,1)S(1)} copy-done((bf16[1,16,64]{2,1,0:T(8,128)(2,1)S(1)}, bf16[1,16,64]{2,1,0:T(8,128)(2,1)}, u32[]{:S(2)}) %copy-start.4) | copy-done | bytes 2072
  7.1 0.0 copy-start.5
  7.1 0.7 %copy-done.5 = s32[1,16]{1,0:T(1,128)S(1)} copy-done((s32[1,16]{1,0:T(1,128)S(1)}, s32[1,16]{1,0:T(1,128)}, u32[]{:S(2)}) %copy-start.5) | copy-done | bytes 88
  7.7 33.5 %shard_map.102 = (bf16[16,2048]{1,0:T(8,128)(2,1)S(1)}, f32[1,1,32]{2,1,0:T(1,128)S(1)}, bf16[64,2048]{1,0:T(8,128)(2,1)S(1)}, bf16[64,2048]{1,0:T(8,128)(2,1)S(...) custom-call(bf16[16,2048]{1,0:T(8,128)(2,1)S(1)} %copy-done.1, bf16[16,2048]{1,0:T(8,128)(2,1)S(1)} %copy-done.2, ...), custom_call_target="tpu_custom_call" | custom-call | flops 1610612736 | bytes 16777216 | tf_op jit(solution)/shard_map/pallas_call | solution.py:429
  41.2 7.8 %shard_map.103 = (bf16[1,2048,2048]{2,1,0:T(8,128)(2,1)}, bf16[1,2048,2048]{2,1,0:T(8,128)(2,1)}) custom-call(bf16[64,2048]{1,0:T(8,128)(2,1)S(1)} %get-tuple-element.13.rows_ref, bf16[64,2048]{1,0:T(8,128)(2,1)S(1)} %get-tuple-element.14.pg_ref, bf16[64,2048]{1,0:T(8,128)(2,1)S(1)} %get-tuple-element.15.hidden_ref, ...), custom_call_target="tpu_custom_call" | custom-call | flops 1073741824 | bytes 16777216 | tf_op jit(solution)/shard_map/pallas_call | solution.py:476
  49.0 0.6 %copy.13 = bf16[16,2048]{1,0:T(8,128)(2,1)} copy(bf16[16,2048]{1,0:T(8,128)(2,1)S(1)} %get-tuple-element.24) | data formatting | bytes 131072
  49.7 0.5 %copy.14 = f32[1,1,32]{2,1,0:T(1,128)} copy(f32[1,1,32]{2,1,0:T(1,128)S(1)} %get-tuple-element.27) | data formatting | bytes 256
Async XLA Ops:
  0.6 3.4 %copy-start = (bf16[1,2048,2048]{2,1,0:T(8,128)(2,1)S(1)}, bf16[1,2048,2048]{2,1,0:T(8,128)(2,1)}, u32[]{:S(2)}) copy-start(bf16[1,2048,2048]{2,1,0:T(8,128)(2,1)} %up_hbm.1) | copy-start | bytes 25165828
  4.0 0.8 %copy-start.1 = (bf16[16,2048]{1,0:T(8,128)(2,1)S(1)}, bf16[16,2048]{1,0:T(8,128)(2,1)}, u32[]{:S(2)}) copy-start(bf16[16,2048]{1,0:T(8,128)(2,1)} %x_ref.1) | copy-start | bytes 196612
  4.9 0.8 %copy-start.2 = (bf16[16,2048]{1,0:T(8,128)(2,1)S(1)}, bf16[16,2048]{1,0:T(8,128)(2,1)}, u32[]{:S(2)}) copy-start(bf16[16,2048]{1,0:T(8,128)(2,1)} %g_ref.1) | copy-start | bytes 196612
  5.7 0.7 %copy-start.3 = (s32[1,16,64]{2,1,0:T(8,128)S(1)}, s32[1,16,64]{2,1,0:T(8,128)}, u32[]{:S(2)}) copy-start(s32[1,16,64]{2,1,0:T(8,128)} %chosen_ref.1) | copy-start | bytes 12292
  6.4 0.7 %copy-start.4 = (bf16[1,16,64]{2,1,0:T(8,128)(2,1)S(1)}, bf16[1,16,64]{2,1,0:T(8,128)(2,1)}, u32[]{:S(2)}) copy-start(bf16[1,16,64]{2,1,0:T(8,128)(2,1)} %gates_ref.1) | copy-start | bytes 6148
  7.1 0.7 %copy-start.5 = (s32[1,16]{1,0:T(1,128)S(1)}, s32[1,16]{1,0:T(1,128)}, u32[]{:S(2)}) copy-start(s32[1,16]{1,0:T(1,128)} %counts_ref.1) | copy-start | bytes 196

commit v2 on v1

--- a/solution.py
+++ b/solution.py
@@ -157,11 +157,11 @@
 
 
 def expert_kernel(
-    x_ref, g_ref, chosen_ref, counts_ref, gates_ref, up_hbm, down_hbm,
-    in_grad_ref, gate_ref, rows_ref, scaled_ref, hidden_ref, pg_ref,
-    up_v, down_v, send, recv, grows, slope, dx_acc, dx_out, dx_in, gate_out, gate_in,
+    x_hbm, g_hbm, chosen_hbm, counts_hbm, gates_hbm, up_hbm, down_hbm,
+    in_grad_ref, gate_ref, rows_hbm, scaled_hbm, hidden_hbm, pg_hbm,
+    rows_ref, scaled_ref, hidden_ref, pg_ref, x_ref, g_ref, chosen_ref, counts_ref, gates_ref, up_v, down_v, send, recv, grows, slope, dx_acc, dx_out, dx_in, gate_out, gate_in,
     ret_send, ret_recv,
-    w_sem, send_sem, recv_sem, fwd_send, fwd_recv, ret_ssem, ret_rsem, pair_send, pair_recv,
+    in_sem, out_sem, w_sem, send_sem, recv_sem, fwd_send, fwd_recv, ret_ssem, ret_rsem, pair_send, pair_recv,
 ):
     tok, width = x_ref.shape
     experts, cap = chosen_ref.shape[1:]
@@ -175,6 +175,20 @@
     core = me % 2
     mate = me + 1 - 2 * core
 
+    small = [
+        pltpu.make_async_copy(src, dst, in_sem.at[i])
+        for i, (src, dst) in enumerate(
+            (
+                (chosen_hbm, chosen_ref),
+                (counts_hbm, counts_ref),
+                (x_hbm, x_ref),
+                (g_hbm, g_ref),
+                (gates_hbm, gates_ref),
+            )
+        )
+    ]
+    for copy in small:
+        copy.start()
     up_copy = pltpu.make_async_copy(up_hbm.at[0], up_v, w_sem.at[0])
     down_copy = pltpu.make_async_copy(down_hbm.at[0], down_v, w_sem.at[1])
     up_copy.start()
@@ -191,6 +205,9 @@
         return 0
 
     lax.fori_loop(1, experts, greet, 0)
+
+    small[0].wait()
+    small[1].wait()
 
     chosen = chosen_ref[0]
     slot = iota((experts, cap), 1)
@@ -225,9 +242,12 @@
         & ((qi & (NB - 1)) == (ql >> log_tok))
     ).astype(jnp.bfloat16)
 
+    small[2].wait()
     pl.semaphore_wait(barrier, experts)
 
     for a, ref in enumerate((x_ref, g_ref)):
+        if a == 1:
+            small[3].wait()
         stacked = jnp.concatenate(
             [ref[:, j * wide:(j + 1) * wide] for j in range(NB)], axis=0
         )
@@ -239,8 +259,8 @@
             pltpu.make_async_remote_copy(
                 src_ref=send.at[a, dst],
                 dst_ref=recv.at[a, core, chip],
-                send_sem=send_sem.at[a, dst],
-                recv_sem=recv_sem.at[a, chip],
+                send_sem=send_sem.at[a],
+                recv_sem=recv_sem.at[a],
                 device_id={"expert": 2 * dst + core},
             ).start()
             return 0
@@ -254,18 +274,10 @@
     ).astype(jnp.bfloat16)
 
     def arrive(a):
-        def one(k, _):
-            src = far(k)
-            pltpu.make_async_remote_copy(
-                src_ref=send.at[a, src],
-                dst_ref=recv.at[a, core, src],
-                send_sem=send_sem.at[a, src],
-                recv_sem=recv_sem.at[a, src],
-                device_id={"expert": 2 * src + core},
-            ).wait()
-            return 0
-
-        lax.fori_loop(1, experts, one, 0)
+        every = pl.ds(0, experts - 1)
+        pltpu.make_async_copy(
+            recv.at[a, core, every], recv.at[a, core, every], recv_sem.at[a]
+        ).wait()
         copy = pltpu.make_async_remote_copy(
             src_ref=recv.at[a, core],
             dst_ref=recv.at[a, core],
@@ -291,6 +303,8 @@
             device_id={"expert": mate},
         )
 
+    small[4].wait()
+
     my_list = chosen_ref[0, pl.ds(chip, 1), :]
     my_gate = gates_ref[0].astype(jnp.float32)
     my_gate = jnp.sum(
@@ -312,7 +326,7 @@
     other_half(0).wait_recv()
     unfold(0, 1 - core, rows_ref)
 
-    step = 512
+    step = 1024
     x_rows = rows_ref[...]
 
     def forward(c, _):
@@ -365,6 +379,19 @@
         send_sem=pair_send.at[1], recv_sem=pair_recv.at[1], device_id={"expert": mate},
     )
     gate_copy.start()
+    keep = [
+        pltpu.make_async_copy(src, dst, out_sem.at[i])
+        for i, (src, dst) in enumerate(
+            (
+                (rows_ref, rows_hbm),
+                (scaled_ref, scaled_hbm),
+                (hidden_ref, hidden_hbm),
+                (pg_ref, pg_hbm),
+            )
+        )
+    ]
+    for copy in keep:
+        copy.start()
     dx_copy.wait()
     both = (
         dx_acc[ours, :].astype(jnp.bfloat16).astype(jnp.float32)
@@ -379,8 +406,8 @@
         pltpu.make_async_remote_copy(
             src_ref=ret_send.at[dst],
             dst_ref=ret_recv.at[chip],
-            send_sem=ret_ssem.at[dst],
-            recv_sem=ret_rsem.at[chip],
+            send_sem=ret_ssem,
+            recv_sem=ret_rsem,
             device_id={"expert": 2 * dst + core},
         ).start()
         return 0
@@ -394,24 +421,27 @@
     fwd_x.wait_send()
     fwd_g.wait_send()
 
-    def taken(k, _):
-        src = far(k)
-        pltpu.make_async_remote_copy(
-            src_ref=ret_send.at[src],
-            dst_ref=ret_recv.at[src],
-            send_sem=ret_ssem.at[src],
-            recv_sem=ret_rsem.at[src],
-            device_id={"expert": 2 * src + core},
-        ).wait()
-        return 0
-
-    lax.fori_loop(1, experts, taken, 0)
+    every = pl.ds(0, experts - 1)
+    pltpu.make_async_copy(ret_recv.at[every], ret_recv.at[every], ret_rsem).wait()
     folded = f32_dot(pick, ret_recv[...].reshape(tall, wide), ((0,), (0,))).astype(jnp.bfloat16)
     for j in range(NB):
         in_grad_ref[:, j * wide:(j + 1) * wide] = folded[j * tok:(j + 1) * tok]
-
-
-def grads_kernel(rows_ref, pg_ref, hidden_ref, scaled_ref, up_ref, down_ref):
+    for copy in keep:
+        copy.wait()
+    for a in range(2):
+        pltpu.make_async_copy(send.at[a, every], send.at[a, every], send_sem.at[a]).wait()
+    pltpu.make_async_copy(ret_send.at[every], ret_send.at[every], ret_ssem).wait()
+
+
+def grads_kernel(
+    rows_ref, pg_ref, hidden_ref, scaled_ref, in_grad_in, gate_in,
+    up_ref, down_ref, in_grad_ref, gate_ref,
+):
+    @pl.when(pl.program_id(0) == 0)
+    def _():
+        in_grad_ref[...] = in_grad_in[...]
+        gate_ref[...] = gate_in[...]
+
     up_ref[0] = f32_dot(rows_ref[...], pg_ref[...], ((0,), (0,))).astype(jnp.bfloat16)
     down_ref[0] = f32_dot(hidden_ref[...], scaled_ref[...], ((0,), (0,))).astype(jnp.bfloat16)
 
@@ -424,7 +454,7 @@
     wide = width // NB
     bf16, f32 = jnp.bfloat16, jnp.float32
     vmem = pl.BlockSpec(memory_space=pltpu.VMEM)
-    hbm = pl.BlockSpec(memory_space=pl.ANY)
+    hbm = pl.BlockSpec(memory_space=pltpu.HBM)
     dma = pltpu.SemaphoreType.DMA
     in_grad, gate_grad, x_rows, scaled, hidden, pre_grad = pl.pallas_call(
         expert_kernel,
@@ -436,9 +466,18 @@
             jax.ShapeDtypeStruct((2 * rows, ff), bf16),
             jax.ShapeDtypeStruct((2 * rows, ff), bf16),
         ),
-        in_specs=[vmem] * 5 + [hbm] * 2,
-        out_specs=(vmem,) * 6,
+        in_specs=[hbm] * 7,
+        out_specs=(vmem,) * 2 + (hbm,) * 4,
         scratch_shapes=[
+            pltpu.VMEM((2 * rows, width), bf16),
+            pltpu.VMEM((2 * rows, width), bf16),
+            pltpu.VMEM((2 * rows, ff), bf16),
+            pltpu.VMEM((2 * rows, ff), bf16),
+            pltpu.VMEM((tok, width), bf16),
+            pltpu.VMEM((tok, width), bf16),
+            pltpu.VMEM(chosen.shape, jnp.int32),
+            pltpu.VMEM(counts.shape, jnp.int32),
+            pltpu.VMEM(gates.shape, bf16),
             pltpu.VMEM((width, ff), bf16),
             pltpu.VMEM((ff, width), bf16),
             pltpu.VMEM((2, experts, HOP, wide), bf16),
@@ -452,18 +491,20 @@
             pltpu.VMEM((8, 128), f32),
             pltpu.VMEM((experts, HOP, wide), bf16),
             pltpu.VMEM((experts, HOP, wide), bf16),
-            dma((2,)),
-            dma((2, experts)),
-            dma((2, experts)),
-            dma((2,)),
-            dma((2,)),
-            dma((experts,)),
-            dma((experts,)),
+            dma((5,)),
+            dma((4,)),
+            dma((2,)),
+            dma((2,)),
+            dma((2,)),
+            dma((2,)),
+            dma((2,)),
+            dma,
+            dma,
             dma((2,)),
             dma((2,)),
         ],
         compiler_params=pltpu.CompilerParams(
-            collective_id=0, has_side_effects=True, vmem_limit_bytes=40 << 20
+            collective_id=0, has_side_effects=True, vmem_limit_bytes=62 << 20
         ),
         cost_estimate=pl.CostEstimate(
             flops=6 * 2 * rows * width * ff,
@@ -472,31 +513,37 @@
         ),
     )(tokens_in, out_grad, chosen, counts, gates, w_up, w_down)
 
-    steps = 8
-    grad_up, grad_down = pl.pallas_call(
+    steps = 4
+    grad_up, grad_down, in_grad, gate_grad = pl.pallas_call(
         grads_kernel,
         grid=(steps,),
         out_shape=(
             jax.ShapeDtypeStruct((1, width, ff), bf16),
             jax.ShapeDtypeStruct((1, ff, width), bf16),
+            jax.ShapeDtypeStruct((tok, width), bf16),
+            jax.ShapeDtypeStruct((1, 1, cap // 2), f32),
         ),
         in_specs=[
             pl.BlockSpec((2 * rows, width // steps), lambda i: (0, i)),
             pl.BlockSpec((2 * rows, ff), lambda i: (0, 0)),
             pl.BlockSpec((2 * rows, ff // steps), lambda i: (0, i)),
             pl.BlockSpec((2 * rows, width), lambda i: (0, 0)),
+            pl.BlockSpec((tok, width), lambda i: (0, 0)),
+            pl.BlockSpec((1, 1, cap // 2), lambda i: (0, 0, 0)),
         ],
         out_specs=(
             pl.BlockSpec((1, width // steps, ff), lambda i: (0, i, 0)),
             pl.BlockSpec((1, ff // steps, width), lambda i: (0, i, 0)),
-        ),
-        compiler_params=pltpu.CompilerParams(vmem_limit_bytes=32 << 20),
+            pl.BlockSpec((tok, width), lambda i: (0, 0)),
+            pl.BlockSpec((1, 1, cap // 2), lambda i: (0, 0, 0)),
+        ),
+        compiler_params=pltpu.CompilerParams(vmem_limit_bytes=62 << 20),
         cost_estimate=pl.CostEstimate(
             flops=8 * rows * width * ff,
             bytes_accessed=4 * width * ff,
             transcendentals=0,
         ),
-    )(x_rows, pre_grad, hidden, scaled)
+    )(x_rows, pre_grad, hidden, scaled, in_grad, gate_grad)
     return in_grad, grad_up, grad_down, gate_grad
 
 

time: 50.5 us -> 40.7 us (0.81)
  local copies, waits for them, and re-layouts: 8.23 us -> 0 us
  Pallas kernels: 41.3 us -> 39.8 us
    unnamed x14 -> x0, local copies, waits for them, and re-layouts: 8.23 us -> none
    pallas_call x1, Pallas kernels: 33.5 us -> 31.9 us  [on_device_pairs(): pl.pallas_call(expert_kernel, out_shape=(jax.ShapeDtypeStruct((tok, width...]
where the time goes in v2:
time: 40.7 us; the launch traced here: 40.4 us
  Pallas kernels  39.8 us (98%)
  between operations  0.64 us (2%)
    pallas_call x1, Pallas kernels, on_device_pairs(): pl.pallas_call(expert_kernel, out_shape=(jax.ShapeDtypeStruct((tok, width...  31.9 us
    pallas_call x1, Pallas kernels, on_device_pairs(): pl.pallas_call(grads_kernel, grid=(steps,), out_shape=(jax.ShapeDtypeStru...  7.89 us

profile of v2, /device:TPU:0, one launch (start us, length us, event | category | flops | bytes accessed | tf_op | source)
XLA Modules:
  0.0 40.4 jit_solution(2644553697386015990)
XLA Ops:
  0.6 31.9 %shard_map.102 = (bf16[16,2048]{1,0:T(8,128)(2,1)}, f32[1,1,32]{2,1,0:T(1,128)}, bf16[64,2048]{1,0:T(8,128)(2,1)}, bf16[64,2048]{1,0:T(8,128)(2,1)}, bf16[64,2048]{1,0:T(8,128)(2,1)}, /*index=5*/bf16[64,2048]{1,0:T(8,128)(2,1)}) custom-call(bf16[16,2048]{1,0:T(8,128)(2,1)} %x_hbm.1, bf16[16,2048]{1,0:T(8,128)(2,1)} %g_hbm.1, s32[1,16,64]{2,1,0:T(8,128)} %chosen_hbm.1, ...), custom_call_target="tpu_custom_call" | custom-call | flops 1610612736 | bytes 16777216 | tf_op jit(solution)/shard_map/pallas_call | solution.py:459
  32.6 7.9 %shard_map.103 = (bf16[1,2048,2048]{2,1,0:T(8,128)(2,1)}, bf16[1,2048,2048]{2,1,0:T(8,128)(2,1)}, bf16[16,2048]{1,0:T(8,128)(2,1)}, f32[1,1,32]{2,1,0:T(1,128)}) custom-call(bf16[64,2048]{1,0:T(8,128)(2,1)} %get-tuple-element.14.rows_ref, bf16[64,2048]{1,0:T(8,128)(2,1)} %get-tuple-element.15.pg_ref, bf16[64,2048]{1,0:T(8,128)(2,1)} %get-tuple-element.16.hidden_ref, ...), custom_call_target="tpu_custom_call" | custom-call | flops 1073741824 | bytes 16777216 | tf_op jit(solution)/shard_map/pallas_call | solution.py:517

commit v3 on v2

--- a/solution.py
+++ b/solution.py
@@ -345,14 +345,12 @@
     unfold(1, 1 - core, grows)
     g_rows = grows[...]
     scaled_ref[...] = (weight * g_rows.astype(jnp.float32)).astype(jnp.bfloat16)
-    dx_acc[...] = jnp.zeros_like(dx_acc)
 
     def backward(c, total):
         cols = pl.ds(pl.multiple_of(c * step, step), step)
         back = f32_dot(g_rows, down_v[cols, :], ((1,), (1,)))
         pre_grad = (weight * back * slope[:, cols]).astype(jnp.bfloat16)
         pg_ref[:, cols] = pre_grad
-        dx_acc[...] += f32_dot(pre_grad, up_v[:, cols], ((1,), (1,)))
         return total + jnp.sum(
             hidden_ref[:, cols].astype(jnp.float32) * back, axis=1, keepdims=True
         )
@@ -363,12 +361,6 @@
 
     theirs = pl.ds(pl.multiple_of((1 - core) * rows, rows), rows)
     ours = pl.ds(pl.multiple_of(core * rows, rows), rows)
-    dx_out[...] = dx_acc[theirs, :].astype(jnp.bfloat16)
-    dx_copy = pltpu.make_async_remote_copy(
-        src_ref=dx_out, dst_ref=dx_in,
-        send_sem=pair_send.at[0], recv_sem=pair_recv.at[0], device_id={"expert": mate},
-    )
-    dx_copy.start()
     low = gate_terms.astype(jnp.bfloat16).astype(jnp.float32)
     by_slot = jnp.sum(seat * low, axis=0, keepdims=True)
     gate_out[...] = jnp.broadcast_to(
@@ -376,7 +368,7 @@
     )
     gate_copy = pltpu.make_async_remote_copy(
         src_ref=gate_out, dst_ref=gate_in,
-        send_sem=pair_send.at[1], recv_sem=pair_recv.at[1], device_id={"expert": mate},
+        send_sem=pair_send.at[2], recv_sem=pair_recv.at[2], device_id={"expert": mate},
     )
     gate_copy.start()
     keep = [
@@ -392,28 +384,45 @@
     ]
     for copy in keep:
         copy.start()
-    dx_copy.wait()
-    both = (
-        dx_acc[ours, :].astype(jnp.bfloat16).astype(jnp.float32)
-        + dx_in[...].astype(jnp.float32)
-    ).astype(jnp.bfloat16)
-    stacked = jnp.concatenate([both[:, j * wide:(j + 1) * wide] for j in range(NB)], axis=0)
-    packed = f32_dot(unpack, stacked, ((0,), (0,))).astype(jnp.bfloat16)
-    ret_send[...] = packed.reshape(experts, HOP, wide)
-
-    def give_back(k, _):
-        dst = far(experts - k)
-        pltpu.make_async_remote_copy(
-            src_ref=ret_send.at[dst],
-            dst_ref=ret_recv.at[chip],
-            send_sem=ret_ssem,
-            recv_sem=ret_rsem,
-            device_id={"expert": 2 * dst + core},
-        ).start()
-        return 0
-
-    lax.fori_loop(1, experts, give_back, 0)
-    ret_recv[chip] = ret_send[chip]
+    part = width // 2
+    thin = part // NB
+    dx_copies = []
+    for h in range(2):
+        cols = slice(h * part, (h + 1) * part)
+        dx_acc[:, cols] = f32_dot(pg_ref[...], up_v[cols, :], ((1,), (1,)))
+        dx_out[h] = dx_acc[theirs, cols].astype(jnp.bfloat16)
+        copy = pltpu.make_async_remote_copy(
+            src_ref=dx_out.at[h], dst_ref=dx_in.at[h],
+            send_sem=pair_send.at[h], recv_sem=pair_recv.at[h], device_id={"expert": mate},
+        )
+        copy.start()
+        dx_copies.append(copy)
+    for h in range(2):
+        cols = slice(h * part, (h + 1) * part)
+        dx_copies[h].wait()
+        both = (
+            dx_acc[ours, cols].astype(jnp.bfloat16).astype(jnp.float32)
+            + dx_in[h].astype(jnp.float32)
+        ).astype(jnp.bfloat16)
+        stacked = jnp.concatenate(
+            [both[:, j * thin:(j + 1) * thin] for j in range(NB)], axis=0
+        )
+        packed = f32_dot(unpack, stacked, ((0,), (0,))).astype(jnp.bfloat16)
+        ret_send[h] = packed.reshape(experts, HOP, thin)
+
+        def give_back(k, _, h=h):
+            dst = far(experts - k)
+            pltpu.make_async_remote_copy(
+                src_ref=ret_send.at[h, dst],
+                dst_ref=ret_recv.at[h, chip],
+                send_sem=ret_ssem.at[h],
+                recv_sem=ret_rsem.at[h],
+                device_id={"expert": 2 * dst + core},
+            ).start()
+            return 0
+
+        lax.fori_loop(1, experts, give_back, 0)
+        ret_recv[h, chip] = ret_send[h, chip]
 
     gate_copy.wait()
     total = gate_out[0:1, :cap] + gate_in[0:1, :cap]
@@ -422,15 +431,23 @@
     fwd_g.wait_send()
 
     every = pl.ds(0, experts - 1)
-    pltpu.make_async_copy(ret_recv.at[every], ret_recv.at[every], ret_rsem).wait()
-    folded = f32_dot(pick, ret_recv[...].reshape(tall, wide), ((0,), (0,))).astype(jnp.bfloat16)
-    for j in range(NB):
-        in_grad_ref[:, j * wide:(j + 1) * wide] = folded[j * tok:(j + 1) * tok]
+    for h in range(2):
+        pltpu.make_async_copy(
+            ret_recv.at[h, every], ret_recv.at[h, every], ret_rsem.at[h]
+        ).wait()
+        folded = f32_dot(
+            pick, ret_recv[h].reshape(tall, thin), ((0,), (0,))
+        ).astype(jnp.bfloat16)
+        for j in range(NB):
+            at = h * part + j * thin
+            in_grad_ref[:, at:at + thin] = folded[j * tok:(j + 1) * tok]
     for copy in keep:
         copy.wait()
     for a in range(2):
         pltpu.make_async_copy(send.at[a, every], send.at[a, every], send_sem.at[a]).wait()
-    pltpu.make_async_copy(ret_send.at[every], ret_send.at[every], ret_ssem).wait()
+        pltpu.make_async_copy(
+            ret_send.at[a, every], ret_send.at[a, every], ret_ssem.at[a]
+        ).wait()
 
 
 def grads_kernel(
@@ -485,12 +502,12 @@
             pltpu.VMEM((2 * rows, width), bf16),
             pltpu.VMEM((2 * rows, ff), f32),
             pltpu.VMEM((2 * rows, width), f32),
-            pltpu.VMEM((rows, width), bf16),
-            pltpu.VMEM((rows, width), bf16),
+            pltpu.VMEM((2, rows, width // 2), bf16),
+            pltpu.VMEM((2, rows, width // 2), bf16),
             pltpu.VMEM((8, 128), f32),
             pltpu.VMEM((8, 128), f32),
-            pltpu.VMEM((experts, HOP, wide), bf16),
-            pltpu.VMEM((experts, HOP, wide), bf16),
+            pltpu.VMEM((2, experts, HOP, wide // 2), bf16),
+            pltpu.VMEM((2, experts, HOP, wide // 2), bf16),
             dma((5,)),
             dma((4,)),
             dma((2,)),
@@ -498,10 +515,10 @@
             dma((2,)),
             dma((2,)),
             dma((2,)),
-            dma,
-            dma,
             dma((2,)),
             dma((2,)),
+            dma((3,)),
+            dma((3,)),
         ],
         compiler_params=pltpu.CompilerParams(
             collective_id=0, has_side_effects=True, vmem_limit_bytes=62 << 20

time: 40.7 us -> 39.5 us (0.971)
  Pallas kernels: 39.8 us -> 38.7 us
    pallas_call x1, Pallas kernels: 31.9 us -> 30.8 us  [on_device_pairs(): pl.pallas_call(expert_kernel, out_shape=(jax.ShapeDtypeStruct((tok, width...]
where the time goes in v3:
time: 39.5 us; the launch traced here: 39.3 us
  Pallas kernels  38.7 us (98%)
  between operations  0.64 us (2%)
    pallas_call x1, Pallas kernels, on_device_pairs(): pl.pallas_call(expert_kernel, out_shape=(jax.ShapeDtypeStruct((tok, width...  30.8 us
    pallas_call x1, Pallas kernels, on_device_pairs(): pl.pallas_call(grads_kernel, grid=(steps,), out_shape=(jax.ShapeDtypeStru...  7.89 us

profile of v3, /device:TPU:0, one launch (start us, length us, event | category | flops | bytes accessed | tf_op | source)
XLA Modules:
  0.0 39.3 jit_solution(4813425791865911392)
XLA Ops:
  0.6 30.8 %shard_map.102 = (bf16[16,2048]{1,0:T(8,128)(2,1)}, f32[1,1,32]{2,1,0:T(1,128)}, bf16[64,2048]{1,0:T(8,128)(2,1)}, bf16[64,2048]{1,0:T(8,128)(2,1)}, bf16[64,2048]{1,0:T(8,128)(2,1)}, /*index=5*/bf16[64,2048]{1,0:T(8,128)(2,1)}) custom-call(bf16[16,2048]{1,0:T(8,128)(2,1)} %x_hbm.1, bf16[16,2048]{1,0:T(8,128)(2,1)} %g_hbm.1, s32[1,16,64]{2,1,0:T(8,128)} %chosen_hbm.1, ...), custom_call_target="tpu_custom_call" | custom-call | flops 1610612736 | bytes 16777216 | tf_op jit(solution)/shard_map/pallas_call | solution.py:476
  31.4 7.9 %shard_map.103 = (bf16[1,2048,2048]{2,1,0:T(8,128)(2,1)}, bf16[1,2048,2048]{2,1,0:T(8,128)(2,1)}, bf16[16,2048]{1,0:T(8,128)(2,1)}, f32[1,1,32]{2,1,0:T(1,128)}) custom-call(bf16[64,2048]{1,0:T(8,128)(2,1)} %get-tuple-element.14.rows_ref, bf16[64,2048]{1,0:T(8,128)(2,1)} %get-tuple-element.15.pg_ref, bf16[64,2048]{1,0:T(8,128)(2,1)} %get-tuple-element.16.hidden_ref, ...), custom_call_target="tpu_custom_call" | custom-call | flops 1073741824 | bytes 16777216 | tf_op jit(solution)/shard_map/pallas_call | solution.py:534
